TPU v7x, 512 devices: a whole 4x8x8 slice. The times are simulated.
512 devices in a mesh: tm: 16 (over y, core), tile: 32 (over z, x).
Axes of the slice: x: 4, y: 8, z: 8, core: 2. Of those that a mesh axis runs over, the one named last changes fastest.
Arguments:
- features: bfloat16 [32, 128, 96, 128], P('tm', 'tile'), may hold values from -6 to 6
- gain_one: float32 [96], replicated, may hold values from 0.1 to 1.9
- gain_two: float32 [96], replicated, may hold values from 0.1 to 1.9
- gain_head: float32 [96], replicated, may hold values from 0.1 to 1.9
- conv_one: bfloat16 [3, 3, 3, 96, 96], replicated, may hold values from -0.125 to 0.125
- conv_two: bfloat16 [3, 3, 3, 96, 96], replicated, may hold values from -0.125 to 0.125
- conv_head: bfloat16 [3, 3, 3, 3, 96], replicated, may hold values from -0.125 to 0.125
Outputs:
- decoded: float32 [32, 128, 3, 128], P('tm', 'tile')
All inputs are finite; a program needn't handle non-finite values.
Results may differ from a plain program's by a relative error of at most 0.009.
Values may be sent and summed in bfloat16 or wider, within the bound.
A program may use at most 128 MiB of HBM per device.

v0:
```python
import jax
import jax.numpy as jnp
from jax import lax
from jax.sharding import PartitionSpec as P


def passed_along(x, axis, by):
    peers = lax.axis_size(axis)
    pairs = [(i, i + by) for i in range(peers) if 0 <= i + by < peers]
    return lax.ppermute(x, axis, pairs)


def with_halo(block, sides, width):
    for axis, dim in sides:
        count = lax.axis_size(axis)
        forward = [(i, i + 1) for i in range(count - 1)]
        backward = [(target, source) for source, target in forward]
        low = lax.ppermute(
            lax.slice_in_dim(block, block.shape[dim] - width, None, axis=dim), axis, forward
        )
        high = lax.ppermute(lax.slice_in_dim(block, 0, width, axis=dim), axis, backward)
        block = jnp.concatenate([low, block, high], axis=dim)
    return block


def activate(values, gains):
    values = values.astype(jnp.float32)
    square = jnp.mean(values * values, axis=2, keepdims=True)
    normed = values * lax.rsqrt(square + 1e-06) * gains[:, None]
    return jax.nn.silu(normed).astype(jnp.bfloat16)


def causal_conv(stacked, kernel, pad_columns=True):
    kernel_depth = kernel.shape[0]
    out_chans = kernel.shape[3]
    in_chans = kernel.shape[4]
    frame_count = stacked.shape[0] - kernel_depth + 1
    row_count = stacked.shape[1] - 2
    padded = jnp.pad(stacked, ((0, 0), (0, 0), (0, 0), (1, 1)))
    columns = padded.shape[3] - 2
    merged = kernel.reshape(kernel_depth, 3, 3 * out_chans, in_chans)
    summed = jnp.zeros((frame_count, row_count, out_chans, columns), jnp.float32)
    for step_t in range(kernel_depth):
        for step_h in range(3):
            product = jnp.einsum(
                "oc,frcw->frow",
                merged[step_t, step_h],
                padded[step_t : step_t + frame_count, step_h : step_h + row_count],
                preferred_element_type=jnp.float32,
            )
            for step_w in range(3):
                summed = (
                    summed
                    + product[
                        :,
                        :,
                        step_w * out_chans : (step_w + 1) * out_chans,
                        step_w : step_w + columns,
                    ]
                )
    return summed


def with_cache(inputs):
    cached = passed_along(inputs, "tm", 1)
    return jnp.concatenate([cached, inputs], axis=0)


def row_rim(inputs):
    return with_halo(inputs, (("tile", 1),), 1)


def local(features, gain_one, gain_two, gain_head, conv_one, conv_two, conv_head):
    first = row_rim(activate(features, gain_one))
    hidden = causal_conv(with_cache(first), conv_one).astype(jnp.bfloat16)
    second = row_rim(activate(hidden, gain_two))
    branch = causal_conv(with_cache(second), conv_two)
    residual_sum = (features.astype(jnp.float32) + branch).astype(jnp.bfloat16)
    head_in = row_rim(activate(residual_sum, gain_head))
    cached = passed_along(head_in, "tm", 1)
    decoded = causal_conv(jnp.concatenate([cached, head_in], axis=0), conv_head)
    return decoded


def solution(mesh):
    placed = (P("tm", "tile", None, None), P(), P(), P(), P(), P(), P())
    return jax.shard_map(
        local, mesh=mesh, in_specs=placed, out_specs=P("tm", "tile", None, None), check_vma=False
    )
```

profile of v0, /device:TPU:230, one launch (start us, length us, event | category | flops | bytes accessed | tf_op | source)
XLA Modules:
  0.0 118.2 jit_solution(8426029107960049589)
XLA Ops:
  0.0 1.1 copy.10
  1.1 0.0 copy-start
  1.1 0.2 fusion.36
  1.3 0.0 copy-start.1
  1.4 1.0 fusion.43
  2.3 5.4 %collective-permute-start = (bf16[2,1,96,128]{2,3,1,0:T(8,128)(2,1)S(1)}, bf16[2,1,96,128]{2,3,1,0:T(8,128)(2,1)S(1)}, u32[]{:S(2)}, u32[]{:S(2)}) collective-permute-start(bf16[2,1,96,128]{2,3,1,0:T(8,128)(2,1)S(1)} %get-tuple-element.13), channel_id=1, source_target_pairs={{0,1},{1,2},{2,3},{3,4},{4,5},{5,6},{6,7},{7,8},{8,9},{9,10},{10,1... | collective-permute-start | bytes 147464 | tf_op jit(solution)/shard_map/ppermute | solution.py:18
  7.7 1.9 %collective-permute-start.1 = (bf16[2,1,96,128]{2,3,1,0:T(8,128)(2,1)S(1)}, bf16[2,1,96,128]{2,3,1,0:T(8,128)(2,1)S(1)}, u32[]{:S(2)}, u32[]{:S(2)}) collective-permute-start(bf16[2,1,96,128]{2,3,1,0:T(8,128)(2,1)S(1)} %get-tuple-element.14), channel_id=1, source_target_pairs={{1,0},{2,1},{3,2},{4,3},{5,4},{6,5},{7,6},{8,7},{9,8},{10,9},{11,1... | collective-permute-start | bytes 147464 | tf_op jit(solution)/shard_map/ppermute | solution.py:21
  9.7 0.0 collective-permute-done
  9.7 7.5 %collective-permute-done.1 = bf16[2,1,96,128]{2,3,1,0:T(8,128)(2,1)S(1)} collective-permute-done((bf16[2,1,96,128]{2,3,1,0:T(8,128)(2,1)S(1)}, bf16[2,1,96,128]{2,3,1,0:T(8,128)(2,1)S(1)}, u32[]{:S(2)}, u32[]{:S(2)}) %collective-permute-start.1) | collective-permute-done | bytes 49184 | tf_op jit(solution)/shard_map/ppermute | solution.py:21
  17.2 0.1 pad_maximum_fusion
  17.3 1.9 %collective-permute-start.2 = (bf16[2,6,96,128]{2,3,1,0:T(8,128)(2,1)S(1)}, bf16[2,6,96,128]{2,3,1,0:T(8,128)(2,1)S(1)}, u32[]{:S(2)}, u32[]{:S(2)}) collective-permute-start(bf16[2,6,96,128]{2,3,1,0:T(8,128)(2,1)S(1)} %pad_maximum_fusion), channel_id=1, source_target_pairs={{0,32},{32,64},{64,96},{96,128},{128,160},{160,192},{192,224},{224... | collective-permute-start | bytes 884744 | tf_op jit(solution)/shard_map/ppermute | solution.py:10
  19.3 8.4 %collective-permute-done.2 = bf16[2,6,96,128]{2,3,1,0:T(8,128)(2,1)S(1)} collective-permute-done((bf16[2,6,96,128]{2,3,1,0:T(8,128)(2,1)S(1)}, bf16[2,6,96,128]{2,3,1,0:T(8,128)(2,1)S(1)}, u32[]{:S(2)}, u32[]{:S(2)}) %collective-permute-start.2) | collective-permute-done | bytes 294944 | tf_op jit(solution)/shard_map/ppermute | solution.py:10
  27.6 0.3 fusion.13
  27.9 0.4 convolution_bitcast_fusion.10
  28.3 0.4 convolution_bitcast_fusion.11
  28.7 0.4 convolution_bitcast_fusion.12
  29.1 1.6 %convolution_bitcast_fusion.13 = f32[2,4,288,130]{2,3,1,0:T(8,128)} fusion(bf16[4,6,96,130]{2,3,1,0:T(8,128)(2,1)S(1)} %fusion.13, bf16[3,3,288,96]{3,2,1,0:T(8,128)(2,1)S(1)} %bitcast.276), kind=kOutput, calls=%fused_computation.16 | convolution fusion | flops 57507840 | bytes 2107392 | tf_op jit(solution)/shard_map/oc,frcw->frow/dot_general | solution.py:45
  30.7 1.6 %convolution_bitcast_fusion.14 = f32[2,4,288,130]{2,3,1,0:T(8,128)} fusion(bf16[4,6,96,130]{2,3,1,0:T(8,128)(2,1)S(1)} %fusion.13, bf16[3,3,288,96]{3,2,1,0:T(8,128)(2,1)S(1)} %bitcast.277), kind=kOutput, calls=%fused_computation.17 | convolution fusion | flops 57507840 | bytes 2107392 | tf_op jit(solution)/shard_map/oc,frcw->frow/dot_general | solution.py:45
  32.3 1.6 %convolution_bitcast_fusion.15 = f32[2,4,288,130]{2,3,1,0:T(8,128)} fusion(bf16[4,6,96,130]{2,3,1,0:T(8,128)(2,1)S(1)} %fusion.13, bf16[3,3,288,96]{3,2,1,0:T(8,128)(2,1)S(1)} %bitcast.278), kind=kOutput, calls=%fused_computation.18 | convolution fusion | flops 57507840 | bytes 2107392 | tf_op jit(solution)/shard_map/oc,frcw->frow/dot_general | solution.py:45
  33.9 1.6 %convolution_bitcast_fusion.16 = f32[2,4,288,130]{2,3,1,0:T(8,128)} fusion(bf16[4,6,96,130]{2,3,1,0:T(8,128)(2,1)S(1)} %fusion.13, bf16[3,3,288,96]{3,2,1,0:T(8,128)(2,1)S(1)} %bitcast.279), kind=kOutput, calls=%fused_computation.19 | convolution fusion | flops 57507840 | bytes 2107392 | tf_op jit(solution)/shard_map/oc,frcw->frow/dot_general | solution.py:45
  35.5 1.6 %convolution_bitcast_fusion.17 = f32[2,4,288,130]{2,3,1,0:T(8,128)} fusion(bf16[4,6,96,130]{2,3,1,0:T(8,128)(2,1)S(1)} %fusion.13, bf16[3,3,288,96]{3,2,1,0:T(8,128)(2,1)S(1)} %bitcast.280), kind=kOutput, calls=%fused_computation.20 | convolution fusion | flops 57507840 | bytes 2107392 | tf_op jit(solution)/shard_map/oc,frcw->frow/dot_general | solution.py:45
  37.1 1.6 %convolution_bitcast_fusion.9 = f32[2,4,288,130]{2,3,1,0:T(8,128)} fusion(bf16[4,6,96,130]{2,3,1,0:T(8,128)(2,1)S(1)} %fusion.13, bf16[3,3,288,96]{3,2,1,0:T(8,128)(2,1)S(1)} %bitcast.281), kind=kOutput, calls=%fused_computation.12 | convolution fusion | flops 57507840 | bytes 2107392 | tf_op jit(solution)/shard_map/oc,frcw->frow/dot_general | solution.py:45
  38.7 9.3 %fusion.20 = (f32[2,4,128]{2,1,0:T(4,128)S(1)}, bf16[2,4,96,128]{2,3,1,0:T(8,128)(2,1)}) fusion(f32[2,4,288,130]{2,3,1,0:T(8,128)} %convolution_bitcast_fusion.9, f32[2,4,288,130]{2,3,1,0:T(8,128)S(1)} %convolution_bitcast_fusion.10, f32[2,4,288,130]{2,3,1,0:T(8,128)S(1)} %convolution_bitcast_fusion.11, ...), kind=kLoop, calls=%fused_computation.57 | loop fusion | flops 2948096 | bytes 10817536 | tf_op jit(solution)/shard_map/reduce_sum | solution.py:28
  48.0 1.2 %fusion.27 = bf16[2,4,96,128]{2,3,1,0:T(8,128)(2,1)S(1)} fusion(bf16[2,4,96,128]{2,3,1,0:T(8,128)(2,1)} %get-tuple-element.8, f32[96]{0:T(128)S(1)} %copy-done.4, f32[2,4,128]{2,1,0:T(4,128)S(1)} %add_rsqrt_fusion.1), kind=kLoop, calls=%fused_computation.64 | loop fusion | flops 786432 | bytes 397696 | tf_op jit(solution)/shard_map/convert_element_type | solution.py:30
  49.3 1.9 %collective-permute-start.3 = (bf16[2,1,96,128]{2,3,1,0:T(8,128)(2,1)S(1)}, bf16[2,1,96,128]{2,3,1,0:T(8,128)(2,1)S(1)}, u32[]{:S(2)}, u32[]{:S(2)}) collective-permute-start(bf16[2,1,96,128]{2,3,1,0:T(8,128)(2,1)S(1)} %get-tuple-element.11), channel_id=1, source_target_pairs={{0,1},{1,2},{2,3},{3,4},{4,5},{5,6},{6,7},{7,8},{8,9},{9,10},{10,1... | collective-permute-start | bytes 147464 | tf_op jit(solution)/shard_map/ppermute | solution.py:18
  51.2 3.9 %collective-permute-start.4 = (bf16[2,1,96,128]{2,3,1,0:T(8,128)(2,1)S(1)}, bf16[2,1,96,128]{2,3,1,0:T(8,128)(2,1)S(1)}, u32[]{:S(2)}, u32[]{:S(2)}) collective-permute-start(bf16[2,1,96,128]{2,3,1,0:T(8,128)(2,1)S(1)} %get-tuple-element.12), channel_id=1, source_target_pairs={{1,0},{2,1},{3,2},{4,3},{5,4},{6,5},{7,6},{8,7},{9,8},{10,9},{11,1... | collective-permute-start | bytes 147464 | tf_op jit(solution)/shard_map/ppermute | solution.py:21
  55.2 0.3 collective-permute-done.3
  55.5 5.2 %collective-permute-done.4 = bf16[2,1,96,128]{2,3,1,0:T(8,128)(2,1)S(1)} collective-permute-done((bf16[2,1,96,128]{2,3,1,0:T(8,128)(2,1)S(1)}, bf16[2,1,96,128]{2,3,1,0:T(8,128)(2,1)S(1)}, u32[]{:S(2)}, u32[]{:S(2)}) %collective-permute-start.4) | collective-permute-done | bytes 49184 | tf_op jit(solution)/shard_map/ppermute | solution.py:21
  60.7 0.1 pad_maximum_fusion.1
  60.8 2.1 %collective-permute-start.5 = (bf16[2,6,96,128]{2,3,1,0:T(8,128)(2,1)S(1)}, bf16[2,6,96,128]{2,3,1,0:T(8,128)(2,1)S(1)}, u32[]{:S(2)}, u32[]{:S(2)}) collective-permute-start(bf16[2,6,96,128]{2,3,1,0:T(8,128)(2,1)S(1)} %pad_maximum_fusion.1), channel_id=1, source_target_pairs={{0,32},{32,64},{64,96},{96,128},{128,160},{160,192},{192,224},{224... | collective-permute-start | bytes 884744 | tf_op jit(solution)/shard_map/ppermute | solution.py:10
  62.9 8.2 %collective-permute-done.5 = bf16[2,6,96,128]{2,3,1,0:T(8,128)(2,1)S(1)} collective-permute-done((bf16[2,6,96,128]{2,3,1,0:T(8,128)(2,1)S(1)}, bf16[2,6,96,128]{2,3,1,0:T(8,128)(2,1)S(1)}, u32[]{:S(2)}, u32[]{:S(2)}) %collective-permute-start.5) | collective-permute-done | bytes 294944 | tf_op jit(solution)/shard_map/ppermute | solution.py:10
  71.1 0.3 fusion.12
  71.4 0.0 copy-done.2
  71.4 0.4 convolution_bitcast_fusion
  71.8 0.4 convolution_bitcast_fusion.1
  72.2 0.4 convolution_bitcast_fusion.2
  72.6 1.6 %convolution_bitcast_fusion.3 = f32[2,4,288,130]{2,3,1,0:T(8,128)} fusion(bf16[4,6,96,130]{2,3,1,0:T(8,128)(2,1)S(1)} %fusion.12, bf16[3,3,288,96]{3,2,1,0:T(8,128)(2,1)S(1)} %bitcast.285), kind=kOutput, calls=%fused_computation.6 | convolution fusion | flops 57507840 | bytes 2107392 | tf_op jit(solution)/shard_map/oc,frcw->frow/dot_general | solution.py:45
  74.2 1.6 %convolution_bitcast_fusion.4 = f32[2,4,288,130]{2,3,1,0:T(8,128)} fusion(bf16[4,6,96,130]{2,3,1,0:T(8,128)(2,1)S(1)} %fusion.12, bf16[3,3,288,96]{3,2,1,0:T(8,128)(2,1)S(1)} %bitcast.286), kind=kOutput, calls=%fused_computation.7 | convolution fusion | flops 57507840 | bytes 2107392 | tf_op jit(solution)/shard_map/oc,frcw->frow/dot_general | solution.py:45
  75.7 1.6 %convolution_bitcast_fusion.5 = f32[2,4,288,130]{2,3,1,0:T(8,128)} fusion(bf16[4,6,96,130]{2,3,1,0:T(8,128)(2,1)S(1)} %fusion.12, bf16[3,3,288,96]{3,2,1,0:T(8,128)(2,1)S(1)} %bitcast.287), kind=kOutput, calls=%fused_computation.8 | convolution fusion | flops 57507840 | bytes 2107392 | tf_op jit(solution)/shard_map/oc,frcw->frow/dot_general | solution.py:45
  77.3 1.6 %convolution_bitcast_fusion.6 = f32[2,4,288,130]{2,3,1,0:T(8,128)} fusion(bf16[4,6,96,130]{2,3,1,0:T(8,128)(2,1)S(1)} %fusion.12, bf16[3,3,288,96]{3,2,1,0:T(8,128)(2,1)S(1)} %bitcast.288), kind=kOutput, calls=%fused_computation.9 | convolution fusion | flops 57507840 | bytes 2107392 | tf_op jit(solution)/shard_map/oc,frcw->frow/dot_general | solution.py:45
  79.0 1.6 %convolution_bitcast_fusion.7 = f32[2,4,288,130]{2,3,1,0:T(8,128)} fusion(bf16[4,6,96,130]{2,3,1,0:T(8,128)(2,1)S(1)} %fusion.12, bf16[3,3,288,96]{3,2,1,0:T(8,128)(2,1)S(1)} %bitcast.289), kind=kOutput, calls=%fused_computation.10 | convolution fusion | flops 57507840 | bytes 2107392 | tf_op jit(solution)/shard_map/oc,frcw->frow/dot_general | solution.py:45
  80.6 1.6 %convolution_bitcast_fusion.8 = f32[2,4,288,130]{2,3,1,0:T(8,128)} fusion(bf16[4,6,96,130]{2,3,1,0:T(8,128)(2,1)S(1)} %fusion.12, bf16[3,3,288,96]{3,2,1,0:T(8,128)(2,1)S(1)} %bitcast.290), kind=kOutput, calls=%fused_computation.11 | convolution fusion | flops 57507840 | bytes 2107392 | tf_op jit(solution)/shard_map/oc,frcw->frow/dot_general | solution.py:45
  82.2 9.5 %fusion.28 = (f32[2,4,128]{2,1,0:T(4,128)S(1)}, bf16[2,4,96,128]{2,3,1,0:T(8,128)(2,1)}) fusion(f32[2,4,288,130]{2,3,1,0:T(8,128)S(1)} %convolution_bitcast_fusion, f32[2,4,288,130]{2,3,1,0:T(8,128)S(1)} %convolution_bitcast_fusion.1, f32[2,4,288,130]{2,3,1,0:T(8,128)S(1)} %convolution_bitcast_fusion.2, f32[2,4,288,130]{2,3,1,0:T(8,128)} %convolution_bitcast_fusion.3, ...), kind=kLoop, calls=%fused_computation.65 | loop fusion | flops 3144704 | bytes 11014144 | tf_op jit(solution)/shard_map/reduce_sum | solution.py:28
  91.7 1.2 %fusion.35 = bf16[2,4,96,128]{2,3,1,0:T(8,128)(2,1)S(1)} fusion(bf16[2,4,96,128]{2,3,1,0:T(8,128)(2,1)} %get-tuple-element.6, f32[96]{0:T(128)S(1)} %copy-done.5, f32[2,4,128]{2,1,0:T(4,128)S(1)} %add_rsqrt_fusion), kind=kLoop, calls=%fused_computation.72 | loop fusion | flops 786432 | bytes 397696 | tf_op jit(solution)/shard_map/convert_element_type | solution.py:30
  92.9 1.9 %collective-permute-start.6 = (bf16[2,1,96,128]{2,3,1,0:T(8,128)(2,1)S(1)}, bf16[2,1,96,128]{2,3,1,0:T(8,128)(2,1)S(1)}, u32[]{:S(2)}, u32[]{:S(2)}) collective-permute-start(bf16[2,1,96,128]{2,3,1,0:T(8,128)(2,1)S(1)} %get-tuple-element.9), channel_id=1, source_target_pairs={{0,1},{1,2},{2,3},{3,4},{4,5},{5,6},{6,7},{7,8},{8,9},{9,10},{10,1... | collective-permute-start | bytes 147464 | tf_op jit(solution)/shard_map/ppermute | solution.py:18
  94.8 3.9 %collective-permute-start.7 = (bf16[2,1,96,128]{2,3,1,0:T(8,128)(2,1)S(1)}, bf16[2,1,96,128]{2,3,1,0:T(8,128)(2,1)S(1)}, u32[]{:S(2)}, u32[]{:S(2)}) collective-permute-start(bf16[2,1,96,128]{2,3,1,0:T(8,128)(2,1)S(1)} %get-tuple-element.10), channel_id=1, source_target_pairs={{1,0},{2,1},{3,2},{4,3},{5,4},{6,5},{7,6},{8,7},{9,8},{10,9},{11,1... | collective-permute-start | bytes 147464 | tf_op jit(solution)/shard_map/ppermute | solution.py:21
  98.7 0.3 collective-permute-done.6
  99.0 5.2 %collective-permute-done.7 = bf16[2,1,96,128]{2,3,1,0:T(8,128)(2,1)S(1)} collective-permute-done((bf16[2,1,96,128]{2,3,1,0:T(8,128)(2,1)S(1)}, bf16[2,1,96,128]{2,3,1,0:T(8,128)(2,1)S(1)}, u32[]{:S(2)}, u32[]{:S(2)}) %collective-permute-start.7) | collective-permute-done | bytes 49184 | tf_op jit(solution)/shard_map/ppermute | solution.py:21
  104.3 0.1 pad_maximum_fusion.2
  104.4 1.9 %collective-permute-start.8 = (bf16[2,6,96,128]{2,3,1,0:T(8,128)(2,1)S(1)}, bf16[2,6,96,128]{2,3,1,0:T(8,128)(2,1)S(1)}, u32[]{:S(2)}, u32[]{:S(2)}) collective-permute-start(bf16[2,6,96,128]{2,3,1,0:T(8,128)(2,1)S(1)} %pad_maximum_fusion.2), channel_id=1, source_target_pairs={{0,32},{32,64},{64,96},{96,128},{128,160},{160,192},{192,224},{224... | collective-permute-start | bytes 884744 | tf_op jit(solution)/shard_map/ppermute | solution.py:10
  106.3 0.0 copy-done.3
  106.4 8.3 %collective-permute-done.8 = bf16[2,6,96,128]{2,3,1,0:T(8,128)(2,1)S(1)} collective-permute-done((bf16[2,6,96,128]{2,3,1,0:T(8,128)(2,1)S(1)}, bf16[2,6,96,128]{2,3,1,0:T(8,128)(2,1)S(1)}, u32[]{:S(2)}, u32[]{:S(2)}) %collective-permute-start.8) | collective-permute-done | bytes 294944 | tf_op jit(solution)/shard_map/ppermute | solution.py:10
  114.7 0.3 select_maximum_fusion
  115.0 0.2 convolution_bitcast_fusion.18
  115.2 0.3 convolution_bitcast_fusion.19
  115.5 0.3 convolution_bitcast_fusion.20
  115.7 0.3 convolution_bitcast_fusion.21
  116.0 0.3 convolution_bitcast_fusion.22
  116.3 0.3 convolution_bitcast_fusion.23
  116.5 0.3 convolution_bitcast_fusion.24
  116.8 0.3 convolution_bitcast_fusion.25
  117.1 0.3 convolution_bitcast_fusion.26
  117.3 0.2 slice_add_fusion.52
  117.6 0.6 copy.21
  (16 shorter events, 0.1 us)
Async XLA Ops:
  1.1 26.8 %copy-start = (bf16[2,4,96,128]{2,3,1,0:T(8,128)(2,1)}, bf16[2,4,96,128]{2,3,1,0:T(8,128)(2,1)S(1)}, u32[]{:S(2)}) copy-start(bf16[2,4,96,128]{2,3,1,0:T(8,128)(2,1)S(1)} %copy.10) | copy-start | bytes 589828
  1.3 26.6 %copy-start.1 = (bf16[3,3,3,96,96]{4,3,2,1,0:T(8,128)(2,1)S(1)}, bf16[3,3,3,96,96]{4,3,2,1,0:T(8,128)(2,1)}, u32[]{:S(2)}) copy-start(bf16[3,3,3,96,96]{4,3,2,1,0:T(8,128)(2,1)} %param.11) | copy-start | bytes 1492996
  2.3 7.3 %collective-permute-start = (bf16[2,1,96,128]{2,3,1,0:T(8,128)(2,1)S(1)}, bf16[2,1,96,128]{2,3,1,0:T(8,128)(2,1)S(1)}, u32[]{:S(2)}, u32[]{:S(2)}) collective-permute-start(bf16[2,1,96,128]{2,3,1,0:T(8,128)(2,1)S(1)} %get-tuple-element.13), channel_id=1, source_target_pairs={{0,1},{1,2},{2,3},{3,4},{4,5},{5,6},{6,7},{7,8},{8,9},{9,10},{10,1... | collective-permute-start | bytes 147464 | tf_op jit(solution)/shard_map/ppermute | solution.py:18
  7.7 9.5 %collective-permute-start.1 = (bf16[2,1,96,128]{2,3,1,0:T(8,128)(2,1)S(1)}, bf16[2,1,96,128]{2,3,1,0:T(8,128)(2,1)S(1)}, u32[]{:S(2)}, u32[]{:S(2)}) collective-permute-start(bf16[2,1,96,128]{2,3,1,0:T(8,128)(2,1)S(1)} %get-tuple-element.14), channel_id=1, source_target_pairs={{1,0},{2,1},{3,2},{4,3},{5,4},{6,5},{7,6},{8,7},{9,8},{10,9},{11,1... | collective-permute-start | bytes 147464 | tf_op jit(solution)/shard_map/ppermute | solution.py:21
  17.3 10.3 %collective-permute-start.2 = (bf16[2,6,96,128]{2,3,1,0:T(8,128)(2,1)S(1)}, bf16[2,6,96,128]{2,3,1,0:T(8,128)(2,1)S(1)}, u32[]{:S(2)}, u32[]{:S(2)}) collective-permute-start(bf16[2,6,96,128]{2,3,1,0:T(8,128)(2,1)S(1)} %pad_maximum_fusion), channel_id=1, source_target_pairs={{0,32},{32,64},{64,96},{96,128},{128,160},{160,192},{192,224},{224... | collective-permute-start | bytes 884744 | tf_op jit(solution)/shard_map/ppermute | solution.py:10
  38.7 9.4 %copy-start.4 = (f32[96]{0:T(128)S(1)}, f32[96]{0:T(128)}, u32[]{:S(2)}) copy-start(f32[96]{0:T(128)} %param.9) | copy-start | bytes 1156
  48.0 23.4 %copy-start.2 = (bf16[3,3,3,96,96]{4,3,2,1,0:T(8,128)(2,1)S(1)}, bf16[3,3,3,96,96]{4,3,2,1,0:T(8,128)(2,1)}, u32[]{:S(2)}) copy-start(bf16[3,3,3,96,96]{4,3,2,1,0:T(8,128)(2,1)} %param.12) | copy-start | bytes 1492996
  49.3 6.2 %collective-permute-start.3 = (bf16[2,1,96,128]{2,3,1,0:T(8,128)(2,1)S(1)}, bf16[2,1,96,128]{2,3,1,0:T(8,128)(2,1)S(1)}, u32[]{:S(2)}, u32[]{:S(2)}) collective-permute-start(bf16[2,1,96,128]{2,3,1,0:T(8,128)(2,1)S(1)} %get-tuple-element.11), channel_id=1, source_target_pairs={{0,1},{1,2},{2,3},{3,4},{4,5},{5,6},{6,7},{7,8},{8,9},{9,10},{10,1... | collective-permute-start | bytes 147464 | tf_op jit(solution)/shard_map/ppermute | solution.py:18
  51.2 9.5 %collective-permute-start.4 = (bf16[2,1,96,128]{2,3,1,0:T(8,128)(2,1)S(1)}, bf16[2,1,96,128]{2,3,1,0:T(8,128)(2,1)S(1)}, u32[]{:S(2)}, u32[]{:S(2)}) collective-permute-start(bf16[2,1,96,128]{2,3,1,0:T(8,128)(2,1)S(1)} %get-tuple-element.12), channel_id=1, source_target_pairs={{1,0},{2,1},{3,2},{4,3},{5,4},{6,5},{7,6},{8,7},{9,8},{10,9},{11,1... | collective-permute-start | bytes 147464 | tf_op jit(solution)/shard_map/ppermute | solution.py:21
  60.8 10.3 %collective-permute-start.5 = (bf16[2,6,96,128]{2,3,1,0:T(8,128)(2,1)S(1)}, bf16[2,6,96,128]{2,3,1,0:T(8,128)(2,1)S(1)}, u32[]{:S(2)}, u32[]{:S(2)}) collective-permute-start(bf16[2,6,96,128]{2,3,1,0:T(8,128)(2,1)S(1)} %pad_maximum_fusion.1), channel_id=1, source_target_pairs={{0,32},{32,64},{64,96},{96,128},{128,160},{160,192},{192,224},{224... | collective-permute-start | bytes 884744 | tf_op jit(solution)/shard_map/ppermute | solution.py:10
  82.2 9.5 %copy-start.5 = (f32[96]{0:T(128)S(1)}, f32[96]{0:T(128)}, u32[]{:S(2)}) copy-start(f32[96]{0:T(128)} %param.10) | copy-start | bytes 1156
  82.2 24.1 %copy-start.3 = (bf16[3,3,3,3,96]{4,3,2,1,0:T(4,128)(2,1)S(1)}, bf16[3,3,3,3,96]{4,3,2,1,0:T(4,128)(2,1)}, u32[]{:S(2)}) copy-start(bf16[3,3,3,3,96]{4,3,2,1,0:T(4,128)(2,1)} %param.13) | copy-start | bytes 46660
  92.9 6.2 %collective-permute-start.6 = (bf16[2,1,96,128]{2,3,1,0:T(8,128)(2,1)S(1)}, bf16[2,1,96,128]{2,3,1,0:T(8,128)(2,1)S(1)}, u32[]{:S(2)}, u32[]{:S(2)}) collective-permute-start(bf16[2,1,96,128]{2,3,1,0:T(8,128)(2,1)S(1)} %get-tuple-element.9), channel_id=1, source_target_pairs={{0,1},{1,2},{2,3},{3,4},{4,5},{5,6},{6,7},{7,8},{8,9},{9,10},{10,1... | collective-permute-start | bytes 147464 | tf_op jit(solution)/shard_map/ppermute | solution.py:18
  94.8 9.5 %collective-permute-start.7 = (bf16[2,1,96,128]{2,3,1,0:T(8,128)(2,1)S(1)}, bf16[2,1,96,128]{2,3,1,0:T(8,128)(2,1)S(1)}, u32[]{:S(2)}, u32[]{:S(2)}) collective-permute-start(bf16[2,1,96,128]{2,3,1,0:T(8,128)(2,1)S(1)} %get-tuple-element.10), channel_id=1, source_target_pairs={{1,0},{2,1},{3,2},{4,3},{5,4},{6,5},{7,6},{8,7},{9,8},{10,9},{11,1... | collective-permute-start | bytes 147464 | tf_op jit(solution)/shard_map/ppermute | solution.py:21
  104.4 10.3 %collective-permute-start.8 = (bf16[2,6,96,128]{2,3,1,0:T(8,128)(2,1)S(1)}, bf16[2,6,96,128]{2,3,1,0:T(8,128)(2,1)S(1)}, u32[]{:S(2)}, u32[]{:S(2)}) collective-permute-start(bf16[2,6,96,128]{2,3,1,0:T(8,128)(2,1)S(1)} %pad_maximum_fusion.2), channel_id=1, source_target_pairs={{0,32},{32,64},{64,96},{96,128},{128,160},{160,192},{192,224},{224... | collective-permute-start | bytes 884744 | tf_op jit(solution)/shard_map/ppermute | solution.py:10
where the time goes:
time: 119 us; the launch traced here: 118 us
  waiting for transfers between devices  43.5 us (37%)
  starting transfers between devices  25 us (21%)
  other arithmetic  23.8 us (20%)
  matrix products  23.8 us (20%)
  local copies, waits for them, and re-layouts  1.8 us (2%)
    ppermute x3, waiting for transfers between devices, passed_along(): return lax.ppermute(x, axis, pairs)  24.9 us
    dot_general x27, matrix products, causal_conv(): jnp.einsum('oc,frcw->frow', merged[step_t, step_h], padded[step_t:step_t...  23.8 us
    reduce_sum x3, other arithmetic, activate(): square = jnp.mean(values * values, axis=2, keepdims=True)  19 us
    ppermute x3, waiting for transfers between devices, with_halo(): lax.ppermute(lax.slice_in_dim(block, 0, width, axis=dim), axis, backward)  18 us
    ppermute x3, starting transfers between devices, with_halo(): lax.ppermute(lax.slice_in_dim(block, 0, width, axis=dim), axis, backward)  9.76 us
    ppermute x3, starting transfers between devices, with_halo(): lax.ppermute(lax.slice_in_dim(block, block.shape[dim] - width, None, axis...  9.25 us
    ppermute x3, starting transfers between devices, passed_along(): return lax.ppermute(x, axis, pairs)  5.94 us
    convert_element_type x3, other arithmetic, activate(): return jax.nn.silu(normed).astype(jnp.bfloat16)  3.38 us
  transfers between devices with their start and end apart: 9, of which 8 were waited for; matrix products, arithmetic and copies ran while one was open for 0% of the time, Pallas kernels for 0%

commit v1 on v0

v1 whole, which is shorter than its diff:
```python
import functools

import jax
import jax.numpy as jnp
from jax import lax
from jax.experimental import pallas as pl
from jax.experimental.pallas import tpu as pltpu
from jax.sharding import PartitionSpec as P

MESH = pl.DeviceIdType.MESH
F32 = jnp.float32
BF16 = jnp.bfloat16


def act(values, gains):
    square = jnp.sum(values * values, axis=0, keepdims=True) * (1.0 / values.shape[0])
    half = values * lax.rsqrt(square + 1e-06) * (gains * 0.5)
    return (half * jnp.tanh(half) + half).astype(BF16)


def shifted_sum(left, middle, right, column):
    width = column.shape[1]
    from_left = jnp.where(column == 0, 0.0, pltpu.roll(left, 1, 1))
    from_right = jnp.where(column == width - 1, 0.0, pltpu.roll(right, width - 1, 1))
    return from_left + middle + from_right


def kernel(
    sizes,
    features_ref,
    gain_one_ref,
    gain_two_ref,
    gain_head_ref,
    conv_one_ref,
    conv_two_ref,
    conv_head_ref,
    out_ref,
    own,
    raw_one,
    raw_two,
    taps_one,
    taps_two,
    taps_head,
    ext_one,
    ext_two,
    part,
    from_time,
    from_side,
    load_sem,
    send_one,
    recv_one,
    send_two,
    recv_two,
    send_head,
    recv_head,
):
    times, tiles, rows, chans, width = sizes
    t, s = lax.axis_index("tm"), lax.axis_index("tile")
    older, newer = t > 0, t < times - 1
    above, below = s > 0, s < tiles - 1

    loads = [
        pltpu.make_async_copy(features_ref, own, load_sem.at[0]),
        pltpu.make_async_copy(conv_one_ref, raw_one, load_sem.at[1]),
        pltpu.make_async_copy(conv_two_ref, raw_two, load_sem.at[2]),
    ]
    for load in loads:
        load.start()

    senders = [
        (older & above, (-1, -1)),
        (older & below, (-1, 1)),
        (above, (0, -1)),
        (below, (0, 1)),
        (older, (-1, 0)),
    ]
    above_one, below_one, newer_one = (flag.astype(jnp.int32) for flag in (above, below, newer))
    receivers = above_one + below_one + newer_one * (1 + above_one + below_one)
    barrier = pltpu.get_barrier_semaphore()
    for there, (dt, ds) in senders:

        @pl.when(there)
        def _():
            pl.semaphore_signal(barrier, inc=1, device_id=(t + dt, s + ds), device_id_type=MESH)

    for ext in (ext_one, ext_two):

        @pl.when(jnp.logical_not(older))
        def _():
            ext[0:2] = jnp.zeros((2, (rows + 2) * chans, width), BF16)

        @pl.when(jnp.logical_not(above))
        def _():
            ext[:, 0:chans] = jnp.zeros((4, chans, width), BF16)

        @pl.when(jnp.logical_not(below))
        def _():
            ext[:, (rows + 1) * chans :] = jnp.zeros((4, chans, width), BF16)

    def spread(gain_ref):
        return jnp.transpose(jnp.broadcast_to(gain_ref[...], (width, chans)))

    gain_one, gain_two, gain_head = spread(gain_one_ref), spread(gain_two_ref), spread(gain_head_ref)
    column = lax.broadcasted_iota(jnp.int32, (chans, width), 1)

    loads[0].wait()
    for f in range(2):
        for r in range(rows):
            ext_one[2 + f, (r + 1) * chans : (r + 2) * chans] = act(own[f, r].astype(F32), gain_one)

    pl.semaphore_wait(barrier, receivers)

    def row(at, frames, count=1):
        return (pl.ds(frames, 2), pl.ds(at * chans, count * chans))

    def exchange(ext, send_sem, recv_sem):
        plan = [
            (newer & above, older & below, (1, -1), row(1, 2), row(rows + 1, 0)),
            (newer & below, older & above, (1, 1), row(rows, 2), row(0, 0)),
            (above, below, (0, -1), row(1, 2), row(rows + 1, 2)),
            (below, above, (0, 1), row(rows, 2), row(0, 2)),
        ] + [(newer, older, (1, 0), row(r + 1, 2), row(r + 1, 0)) for r in range(rows)]
        return [
            (
                to,
                came,
                pltpu.make_async_remote_copy(
                    src_ref=ext.at[source],
                    dst_ref=ext.at[target],
                    send_sem=send_sem.at[i],
                    recv_sem=recv_sem.at[i],
                    device_id=(t + dt, s + ds),
                    device_id_type=MESH,
                ),
            )
            for i, (to, came, (dt, ds), source, target) in enumerate(plan)
        ]

    def start(copies):
        for to, _, copy in copies:
            pl.when(to)(copy.start)

    def arrive(copies):
        for _, came, copy in copies:
            pl.when(came)(copy.wait_recv)

    def leave(copies):
        for to, _, copy in copies:
            pl.when(to)(copy.wait_send)

    first_copies = exchange(ext_one, send_one, recv_one)
    start(first_copies)

    loads[1].wait()
    for k in range(9):
        taps_one[:, k * chans : (k + 1) * chans] = raw_one[k]
    loads[2].wait()
    for k in range(9):
        taps_two[:, k * chans : (k + 1) * chans] = raw_two[k]
    taps_head[...] = jnp.zeros_like(taps_head)
    for c in range(3):
        for b in range(3):
            for target in range(4):
                for f in range(2):
                    a = f + 2 - target
                    if 0 <= a <= 2:
                        at = ((c * 3 + b) * 2 + target // 2) * 8 + (target % 2) * 4
                        taps_head[at : at + 3, f * chans : (f + 1) * chans] = conv_head_ref[a, b, c].astype(F32)
    head_weights = taps_head[...].astype(BF16)

    def conv_row(taps, ext, r):
        stacks = [
            jnp.concatenate([ext[f + a, r * chans : (r + 3) * chans] for a in range(3)], axis=0) for f in range(2)
        ]
        product = jnp.dot(taps[...], jnp.concatenate(stacks, axis=1), preferred_element_type=F32)
        return [
            shifted_sum(
                *[product[c * chans : (c + 1) * chans, f * width : (f + 1) * width] for c in range(3)], column
            )
            for f in range(2)
        ]

    arrive(first_copies)
    second_copies = exchange(ext_two, send_two, recv_two)
    sent_with = {0: (0, 2, 4), 1: (5,), 2: (6,), rows - 1: (1, 3, 7)}
    for r in (0, rows - 1, 1, 2):
        for f, hidden in enumerate(conv_row(taps_one, ext_one, r)):
            hidden = hidden.astype(BF16).astype(F32)
            ext_two[2 + f, (r + 1) * chans : (r + 2) * chans] = act(hidden, gain_two)
        start([second_copies[i] for i in sent_with[r]])

    arrive(second_copies)
    summed = {}
    lane = lax.broadcasted_iota(jnp.int32, (8, width), 1)
    for pair in range(rows // 2):
        inputs = []
        for r in (2 * pair, 2 * pair + 1):
            branch = conv_row(taps_two, ext_two, r)
            heads = []
            for f in range(2):
                total = (own[f, r].astype(F32) + branch[f]).astype(BF16).astype(F32)
                heads.append(act(total, gain_head))
            inputs.append(jnp.concatenate(heads, axis=0))
        product = jnp.dot(head_weights, jnp.concatenate(inputs, axis=1), preferred_element_type=F32)
        for i in range(2):
            for c in range(3):
                for b in range(3):
                    for late in range(2):
                        at = ((c * 3 + b) * 2 + late) * 8
                        piece = product[at : at + 8, i * width : (i + 1) * width]
                        key = (late, 2 * pair + i + 2 - b, c)
                        summed[key] = summed[key] + piece if key in summed else piece
    for late in range(2):
        for r in range(rows + 2):
            part[late, r] = shifted_sum(*[summed[late, r, c] for c in range(3)], lane)

    plan = [
        (newer & above, older & below, (1, -1), part.at[1, 0], from_side.at[0]),
        (newer & below, older & above, (1, 1), part.at[1, rows + 1], from_side.at[1]),
        (above, below, (0, -1), part.at[0, 0], from_side.at[2]),
        (below, above, (0, 1), part.at[0, rows + 1], from_side.at[3]),
        (newer, older, (1, 0), part.at[1, pl.ds(1, rows)], from_time),
    ]
    head_copies = [
        (
            to,
            came,
            pltpu.make_async_remote_copy(
                src_ref=source,
                dst_ref=target,
                send_sem=send_head.at[i],
                recv_sem=recv_head.at[i],
                device_id=(t + dt, s + ds),
                device_id_type=MESH,
            ),
        )
        for i, (to, came, (dt, ds), source, target) in enumerate(plan)
    ]
    start(head_copies)

    for i, (_, came, _) in enumerate(head_copies):

        @pl.when(jnp.logical_not(came))
        def _():
            if i < 4:
                from_side[i] = jnp.zeros((8, width), F32)
            else:
                from_time[...] = jnp.zeros((rows, 8, width), F32)

    arrive(head_copies)
    for r in range(rows):
        total = part[0, r + 1] + from_time[r]
        if r == rows - 1:
            total = total + from_side[0] + from_side[2]
        if r == 0:
            total = total + from_side[1] + from_side[3]
        for f in range(2):
            for o in range(3):
                out_ref[f, o, r : r + 1] = total[4 * f + o : 4 * f + o + 1]

    leave(first_copies)
    leave(second_copies)
    leave(head_copies)


def local(times, tiles, features, gain_one, gain_two, gain_head, conv_one, conv_two, conv_head):
    frames, rows, chans, width = features.shape
    anywhere = pl.BlockSpec(memory_space=pl.ANY)
    vmem = pl.BlockSpec(memory_space=pltpu.VMEM)
    ext = pltpu.VMEM((4, (rows + 2) * chans, width), BF16)
    raw = pltpu.VMEM((9, 3 * chans, chans), BF16)
    taps = pltpu.VMEM((3 * chans, 9 * chans), BF16)
    dma = pltpu.SemaphoreType.DMA
    decoded = pl.pallas_call(
        functools.partial(kernel, (times, tiles, rows, chans, width)),
        out_shape=jax.ShapeDtypeStruct((frames, 3, rows, width), F32),
        in_specs=[anywhere, vmem, vmem, vmem, anywhere, anywhere, vmem],
        out_specs=vmem,
        scratch_shapes=[
            pltpu.VMEM(features.shape, BF16),
            raw,
            raw,
            taps,
            taps,
            pltpu.VMEM((144, 2 * chans), F32),
            ext,
            ext,
            pltpu.VMEM((2, rows + 2, 8, width), F32),
            pltpu.VMEM((rows, 8, width), F32),
            pltpu.VMEM((4, 8, width), F32),
            dma((3,)),
            dma((8,)),
            dma((8,)),
            dma((8,)),
            dma((8,)),
            dma((5,)),
            dma((5,)),
        ],
        compiler_params=pltpu.CompilerParams(
            collective_id=0, has_side_effects=True, vmem_limit_bytes=48 * 1024 * 1024
        ),
        cost_estimate=pl.CostEstimate(flops=1_100_000_000, bytes_accessed=1_300_000, transcendentals=400_000),
        name="decode",
    )(
        features,
        gain_one.reshape(1, chans),
        gain_two.reshape(1, chans),
        gain_head.reshape(1, chans),
        conv_one.reshape(9, 3 * chans, chans),
        conv_two.reshape(9, 3 * chans, chans),
        conv_head,
    )
    return jnp.transpose(decoded, (0, 2, 1, 3))


def solution(mesh):
    placed = (P("tm", "tile", None, None), P(), P(), P(), P(), P(), P())
    return jax.shard_map(
        functools.partial(local, mesh.shape["tm"], mesh.shape["tile"]),
        mesh=mesh,
        in_specs=placed,
        out_specs=P("tm", "tile", None, None),
        check_vma=False,
    )
```

time: 119 us -> 29.7 us (0.25)
  waiting for transfers between devices: 43.5 us -> 0 us
  starting transfers between devices: 25 us -> 0 us
  Pallas kernels: 0 us -> 24.3 us
  matrix products: 23.8 us -> 0 us
  other arithmetic: 23.8 us -> 0 us
  local copies, waits for them, and re-layouts: 1.8 us -> 5.13 us
    ppermute x9 -> x0, waiting for transfers between devices: 43.5 us -> none  [the longest x3 24.9 us: passed_along(): return lax.ppermute(x, axis, pairs)]
    ppermute x9 -> x0, starting transfers between devices: 25 us -> none  [the longest x3 9.76 us: with_halo(): lax.ppermute(lax.slice_in_dim(block, 0, width, axis=dim), axis, backward)]
    pallas_call x0 -> x1, Pallas kernels: none -> 24.3 us  [local(): pl.pallas_call(functools.partial(kernel, (times, tiles, rows, chans, widt...]
    dot_general x27 -> x0, matrix products: 23.8 us -> none  [causal_conv(): jnp.einsum('oc,frcw->frow', merged[step_t, step_h], padded[step_t:step_t...]
    reduce_sum x3 -> x0, other arithmetic: 19 us -> none  [activate(): square = jnp.mean(values * values, axis=2, keepdims=True)]
    unnamed x14 -> x15, local copies, waits for them, and re-layouts: 1.13 us -> 5.13 us
    convert_element_type x3 -> x0, other arithmetic: 3.38 us -> none  [activate(): return jax.nn.silu(normed).astype(jnp.bfloat16)]
  transfers between devices with their start and end apart: 9 -> 0, of which waited for: 8 -> 0; matrix products, arithmetic and copies ran while one was open for 0% -> 0% of each run, Pallas kernels for 0% -> 0%
where the time goes in v1:
time: 29.7 us; the launch traced here: 29.4 us
  Pallas kernels  24.3 us (82%)
  local copies, waits for them, and re-layouts  5.13 us (17%)
    pallas_call x1, Pallas kernels, local(): pl.pallas_call(functools.partial(kernel, (times, tiles, rows, chans, widt...  24.3 us
    unnamed x15, local copies, waits for them, and re-layouts  5.13 us

profile of v1, /device:TPU:230, one launch (start us, length us, event | category | flops | bytes accessed | tf_op | source)
XLA Modules:
  0.0 29.4 jit_solution(18356073636268469399)
XLA Ops:
  0.0 0.0 copy-start.4
  0.0 0.0 copy-start.5
  0.0 0.0 copy-start.6
  0.0 0.6 %copy-done.4 = f32[96]{0:T(128)S(1)} copy-done((f32[96]{0:T(128)S(1)}, f32[96]{0:T(128)}, u32[]{:S(2)}) %copy-start.4) | copy-done | bytes 408
  0.7 0.0 copy-done.5
  0.7 0.0 copy-done.6
  0.7 0.0 copy-start
  0.7 1.1 %copy-done = bf16[3,3,3,96,96]{4,3,2,1,0:T(8,128)(2,1)S(1)} copy-done((bf16[3,3,3,96,96]{4,3,2,1,0:T(8,128)(2,1)S(1)}, bf16[3,3,3,96,96]{4,3,2,1,0:T(8,128)(2,1)}, u32[]{:S(2)}) %copy-start) | copy-done | bytes 497688
  1.8 0.0 copy-start.1
  1.8 1.1 %copy-done.1 = bf16[3,3,3,96,96]{4,3,2,1,0:T(8,128)(2,1)S(1)} copy-done((bf16[3,3,3,96,96]{4,3,2,1,0:T(8,128)(2,1)S(1)}, bf16[3,3,3,96,96]{4,3,2,1,0:T(8,128)(2,1)}, u32[]{:S(2)}) %copy-start.1) | copy-done | bytes 497688
  2.9 0.0 copy-start.2
  2.9 0.9 %copy-done.2 = bf16[2,4,96,128]{3,2,1,0:T(8,128)(2,1)S(1)} copy-done((bf16[2,4,96,128]{3,2,1,0:T(8,128)(2,1)S(1)}, bf16[2,4,96,128]{3,2,1,0:T(8,128)(2,1)}, u32[]{:S(2)}) %copy-start.2) | copy-done | bytes 196632
  3.8 0.0 copy-start.3
  3.8 0.7 %copy-done.3 = bf16[3,3,3,3,96]{4,3,2,1,0:T(4,128)(2,1)S(1)} copy-done((bf16[3,3,3,3,96]{4,3,2,1,0:T(4,128)(2,1)S(1)}, bf16[3,3,3,3,96]{4,3,2,1,0:T(4,128)(2,1)}, u32[]{:S(2)}) %copy-start.3) | copy-done | bytes 15576
  4.5 24.3 %decode.1 = f32[2,3,4,128]{3,2,1,0:T(4,128)S(1)} custom-call(bf16[2,4,96,128]{3,2,1,0:T(8,128)(2,1)S(1)} %copy-done.2, f32[1,96]{1,0:T(1,128)S(1)} %bitcast.9, f32[1,96]{1,0:T(1,128)S(1)} %bitcast.10, f32[1,96]{1,0:T(1,128)S(1)} %bitcast.11, bf16[9,288,96]{2,1,0:T(8,128)(2,1)S(1)} %bitcast.7, bf16[9,288,96]{2,1,0:T(8,128)(2,1)S(1)} %bitcast.8, ...), custom_call_target="tpu_custom_call" | custom-call | flops 1100000000 | bytes 1300000 | tf_op jit(solution)/shard_map/decode/pallas_call | solution.py:274
  28.8 0.6 %copy.9 = f32[2,4,3,128]{3,1,2,0:T(4,128)} copy(f32[2,4,3,128]{3,1,2,0:T(4,128)S(1)} %bitcast.6) | data formatting | bytes 24576
Async XLA Ops:
  0.0 0.7 %copy-start.4 = (f32[96]{0:T(128)S(1)}, f32[96]{0:T(128)}, u32[]{:S(2)}) copy-start(f32[96]{0:T(128)} %param.8) | copy-start | bytes 1156
  0.0 0.7 %copy-start.5 = (f32[96]{0:T(128)S(1)}, f32[96]{0:T(128)}, u32[]{:S(2)}) copy-start(f32[96]{0:T(128)} %param.9) | copy-start | bytes 1156
  0.0 0.7 %copy-start.6 = (f32[96]{0:T(128)S(1)}, f32[96]{0:T(128)}, u32[]{:S(2)}) copy-start(f32[96]{0:T(128)} %param.10) | copy-start | bytes 1156
  0.7 1.1 %copy-start = (bf16[3,3,3,96,96]{4,3,2,1,0:T(8,128)(2,1)S(1)}, bf16[3,3,3,96,96]{4,3,2,1,0:T(8,128)(2,1)}, u32[]{:S(2)}) copy-start(bf16[3,3,3,96,96]{4,3,2,1,0:T(8,128)(2,1)} %param.11) | copy-start | bytes 1492996
  1.8 1.1 %copy-start.1 = (bf16[3,3,3,96,96]{4,3,2,1,0:T(8,128)(2,1)S(1)}, bf16[3,3,3,96,96]{4,3,2,1,0:T(8,128)(2,1)}, u32[]{:S(2)}) copy-start(bf16[3,3,3,96,96]{4,3,2,1,0:T(8,128)(2,1)} %param.12) | copy-start | bytes 1492996
  2.9 0.9 %copy-start.2 = (bf16[2,4,96,128]{3,2,1,0:T(8,128)(2,1)S(1)}, bf16[2,4,96,128]{3,2,1,0:T(8,128)(2,1)}, u32[]{:S(2)}) copy-start(bf16[2,4,96,128]{3,2,1,0:T(8,128)(2,1)} %features_ref.1) | copy-start | bytes 589828
  3.8 0.7 %copy-start.3 = (bf16[3,3,3,3,96]{4,3,2,1,0:T(4,128)(2,1)S(1)}, bf16[3,3,3,3,96]{4,3,2,1,0:T(4,128)(2,1)}, u32[]{:S(2)}) copy-start(bf16[3,3,3,3,96]{4,3,2,1,0:T(4,128)(2,1)} %conv_head_ref.1) | copy-start | bytes 46660

commit v2 on v1

v2 whole, which is shorter than its diff:
```python
import functools

import jax
import jax.numpy as jnp
from jax import lax
from jax.experimental import pallas as pl
from jax.experimental.pallas import tpu as pltpu
from jax.sharding import PartitionSpec as P

MESH = pl.DeviceIdType.MESH
F32 = jnp.float32
BF16 = jnp.bfloat16


def act(values, gains):
    square = jnp.sum(values * values, axis=0, keepdims=True) * (1.0 / values.shape[0])
    half = values * lax.rsqrt(square + 1e-06) * (gains * 0.5)
    return (half * jnp.tanh(half) + half).astype(BF16)


def shifted_sum(left, middle, right, column):
    width = column.shape[1]
    from_left = jnp.where(column == 0, 0.0, pltpu.roll(left, 1, 1))
    from_right = jnp.where(column == width - 1, 0.0, pltpu.roll(right, width - 1, 1))
    return from_left + middle + from_right


def kernel(
    sizes,
    features_ref,
    gain_one_hbm,
    gain_two_hbm,
    gain_head_hbm,
    conv_one_ref,
    conv_two_ref,
    conv_head_hbm,
    out_ref,
    own,
    gain_one_ref,
    gain_two_ref,
    gain_head_ref,
    conv_head_ref,
    raw_one,
    raw_two,
    taps_one,
    taps_two,
    taps_head,
    ext_one,
    ext_two,
    part,
    from_time,
    from_side,
    load_sem,
    send_one,
    recv_one,
    send_two,
    recv_two,
    send_head,
    recv_head,
):
    times, tiles, rows, chans, width = sizes
    t, s = lax.axis_index("tm"), lax.axis_index("tile")
    older, newer = t > 0, t < times - 1
    above, below = s > 0, s < tiles - 1

    senders = [
        (older & above, (-1, -1)),
        (older & below, (-1, 1)),
        (above, (0, -1)),
        (below, (0, 1)),
        (older, (-1, 0)),
    ]
    above_one, below_one, newer_one = (flag.astype(jnp.int32) for flag in (above, below, newer))
    receivers = above_one + below_one + newer_one * (1 + above_one + below_one)
    barrier = pltpu.get_barrier_semaphore()
    for there, (dt, ds) in senders:

        @pl.when(there)
        def _():
            pl.semaphore_signal(barrier, inc=1, device_id=(t + dt, s + ds), device_id_type=MESH)

    loads = [
        pltpu.make_async_copy(source, target, load_sem.at[i])
        for i, (source, target) in enumerate(
            (
                (features_ref, own),
                (gain_one_hbm, gain_one_ref),
                (gain_two_hbm, gain_two_ref),
                (gain_head_hbm, gain_head_ref),
                (conv_one_ref, raw_one),
                (conv_two_ref, raw_two),
                (conv_head_hbm, conv_head_ref),
            )
        )
    ]
    for load in loads:
        load.start()

    for ext in (ext_one, ext_two):

        @pl.when(jnp.logical_not(older))
        def _():
            ext[0:2] = jnp.zeros((2, (rows + 2) * chans, width), BF16)

        @pl.when(jnp.logical_not(above))
        def _():
            ext[:, 0:chans] = jnp.zeros((4, chans, width), BF16)

        @pl.when(jnp.logical_not(below))
        def _():
            ext[:, (rows + 1) * chans :] = jnp.zeros((4, chans, width), BF16)

    upwards = lax.rem(s, 4) < 2
    near, far = jnp.where(upwards, 1, -1), jnp.where(upwards, -1, 1)
    order = [jnp.where(upwards, rows - 1 - i, i) for i in range(rows)]
    turns = [0, rows - 1, *range(1, rows - 1)]

    def rows_at(at, count=1):
        return pl.ds(pl.multiple_of(at * chans, 32), count * chans)

    def spread(gain_ref):
        return jnp.transpose(jnp.broadcast_to(gain_ref[...], (width, chans)))

    def exists(side):
        return jnp.where(side < 0, s > 0, s < tiles - 1)

    def remote(source, target, send_sem, recv_sem, device):
        return pltpu.make_async_remote_copy(
            src_ref=source,
            dst_ref=target,
            send_sem=send_sem,
            recv_sem=recv_sem,
            device_id=device,
            device_id_type=MESH,
        )

    def edge(ext, sems, side, later):
        source, target = jnp.where(side < 0, 1, rows), jnp.where(side < 0, rows + 1, 0)
        which = jnp.where(side < 0, 0, 1) + 2 * later
        return remote(
            ext.at[pl.ds(2, 2), rows_at(source)],
            ext.at[pl.ds(2 - 2 * later, 2), rows_at(target)],
            sems[0].at[which],
            sems[1].at[which],
            (t + later, s + side),
        )

    def onward(ext, sems, r):
        return remote(
            ext.at[pl.ds(2, 2), rows_at(r + 1)],
            ext.at[pl.ds(0, 2), rows_at(r + 1)],
            sems[0].at[4 + r],
            sems[1].at[4 + r],
            (t + 1, s),
        )

    odd = lax.rem(t, 2) == 1

    def send_both(copy, side):
        pl.when(newer & exists(side) & odd)(copy(side, 1).start)
        pl.when(exists(side))(copy(side, 0).start)
        pl.when(newer & exists(side) & jnp.logical_not(odd))(copy(side, 1).start)

    def send_edge(ext, sems, side):
        send_both(functools.partial(edge, ext, sems), side)

    def send_onward(ext, sems, r):
        pl.when(newer)(onward(ext, sems, r).start)

    def await_edge(ext, sems, side):
        pl.when(exists(side))(edge(ext, sems, -side, 0).wait_recv)
        pl.when(older & exists(side))(edge(ext, sems, -side, 1).wait_recv)

    def await_onward(ext, sems, r):
        pl.when(older)(onward(ext, sems, r).wait_recv)

    def await_row(ext, sems, i):
        if i == 0:
            await_onward(ext, sems, order[0])
            await_onward(ext, sems, order[1])
            await_edge(ext, sems, near)
        elif i == rows - 1:
            for r in order[2:]:
                await_onward(ext, sems, r)
            await_edge(ext, sems, far)

    def drain(ext, sems):
        for side in (near, far):
            pl.when(exists(side))(edge(ext, sems, side, 0).wait_send)
            pl.when(newer & exists(side))(edge(ext, sems, side, 1).wait_send)
        for r in order:
            pl.when(newer)(onward(ext, sems, r).wait_send)

    sems_one, sems_two = (send_one, recv_one), (send_two, recv_two)
    column = lax.broadcasted_iota(jnp.int32, (chans, width), 1)

    def first_act(r, gain):
        for f in range(2):
            ext_one[2 + f, rows_at(r + 1)] = act(own[f, r].astype(F32), gain)

    for load in loads[1:4]:
        load.wait()
    gain_one = spread(gain_one_ref)
    loads[0].wait()
    first_act(order[-1], gain_one)
    first_act(order[0], gain_one)
    pl.semaphore_wait(barrier, receivers)
    for side in (far, near):
        send_edge(ext_one, sems_one, side)
    send_onward(ext_one, sems_one, order[0])
    for i in range(1, rows):
        if i < rows - 1:
            first_act(order[i], gain_one)
        send_onward(ext_one, sems_one, order[i])
    gain_two, gain_head = spread(gain_two_ref), spread(gain_head_ref)

    loads[4].wait()
    for k in range(9):
        taps_one[:, k * chans : (k + 1) * chans] = raw_one[k]
    loads[5].wait()
    for k in range(9):
        taps_two[:, k * chans : (k + 1) * chans] = raw_two[k]
    loads[6].wait()
    taps_head[...] = jnp.zeros_like(taps_head)
    for b in range(3):
        step = jnp.where(upwards, 2 - b, b)
        for a in range(3):
            for c in range(3):
                piece = conv_head_ref[a, step, c].astype(F32)
                for f in range(2):
                    target = f + 2 - a
                    at = ((c * 3 + b) * 2 + target // 2) * 8 + (target % 2) * 4
                    taps_head[at : at + 3, f * chans : (f + 1) * chans] = piece
    head_weights = taps_head[...].astype(BF16)

    def conv_row(taps, ext, r):
        stacks = [jnp.concatenate([ext[f + a, rows_at(r, 3)] for a in range(3)], axis=0) for f in range(2)]
        product = jnp.dot(taps[...], jnp.concatenate(stacks, axis=1), preferred_element_type=F32)
        return [
            shifted_sum(
                *[product[c * chans : (c + 1) * chans, f * width : (f + 1) * width] for c in range(3)], column
            )
            for f in range(2)
        ]

    for i in turns:
        r = order[i]
        await_row(ext_one, sems_one, i)
        for f, hidden in enumerate(conv_row(taps_one, ext_one, r)):
            hidden = hidden.astype(BF16).astype(F32)
            ext_two[2 + f, rows_at(r + 1)] = act(hidden, gain_two)
        if i == 0:
            send_edge(ext_two, sems_two, near)
        if i == rows - 1:
            send_edge(ext_two, sems_two, far)
        send_onward(ext_two, sems_two, r)

    def head_edge(side, later):
        at = jnp.where(side == near, 0, rows + 1)
        which = jnp.where(side < 0, 0, 1) + 2 * later
        return remote(
            part.at[later, at], from_side.at[which], send_head.at[which], recv_head.at[which], (t + later, s + side)
        )

    head_onward = remote(part.at[1, pl.ds(1, rows)], from_time, send_head.at[4], recv_head.at[4], (t + 1, s))

    for side in (near, far):
        for later in range(2):
            sent = exists(side) & older if later else exists(side)

            @pl.when(jnp.logical_not(sent))
            def _():
                from_side[jnp.where(side < 0, 1, 0) + 2 * later] = jnp.zeros((8, width), F32)

    @pl.when(jnp.logical_not(older))
    def _():
        from_time[...] = jnp.zeros((rows, 8, width), F32)

    summed = {}
    lane = lax.broadcasted_iota(jnp.int32, (8, width), 1)

    def settle(place):
        for late in range(2):
            part[late, place] = shifted_sum(*[summed[late, place, c] for c in range(3)], lane)

    for i in turns:
        r = order[i]
        await_row(ext_two, sems_two, i)
        branch = conv_row(taps_two, ext_two, r)
        heads = []
        for f in range(2):
            total = (own[f, r].astype(F32) + branch[f]).astype(BF16).astype(F32)
            heads.append(act(total, gain_head))
        product = jnp.dot(head_weights, jnp.concatenate(heads, axis=0), preferred_element_type=F32)
        for c in range(3):
            for b in range(3):
                for late in range(2):
                    at = ((c * 3 + b) * 2 + late) * 8
                    piece = product[at : at + 8]
                    key = (late, i + 2 - b, c)
                    summed[key] = summed[key] + piece if key in summed else piece
        if i == 0:
            settle(0)
            send_both(head_edge, near)
        if i == rows - 1:
            settle(rows + 1)
            send_both(head_edge, far)
    for place in range(1, rows + 1):
        settle(place)
    pl.when(newer)(head_onward.start)

    drain(ext_one, sems_one)
    drain(ext_two, sems_two)
    pl.when(older)(head_onward.wait_recv)
    for i, r in enumerate(order):
        total = part[0, i + 1] + from_time[i]
        for at, side in ((0, near), (rows - 1, far)):
            if i == at:
                pl.when(exists(side))(head_edge(-side, 0).wait_recv)
                pl.when(older & exists(side))(head_edge(-side, 1).wait_recv)
                came = jnp.where(side < 0, 1, 0)
                total = total + from_side[came] + from_side[came + 2]
        for f in range(2):
            for o in range(3):
                out_ref[f, o, pl.ds(r, 1)] = total[4 * f + o : 4 * f + o + 1]

    for side in (near, far):
        pl.when(exists(side))(head_edge(side, 0).wait_send)
        pl.when(newer & exists(side))(head_edge(side, 1).wait_send)
    pl.when(newer)(head_onward.wait_send)


def local(times, tiles, features, gain_one, gain_two, gain_head, conv_one, conv_two, conv_head):
    frames, rows, chans, width = features.shape
    anywhere = pl.BlockSpec(memory_space=pl.ANY)
    vmem = pl.BlockSpec(memory_space=pltpu.VMEM)
    ext = pltpu.VMEM((4, (rows + 2) * chans, width), BF16)
    raw = pltpu.VMEM((9, 3 * chans, chans), BF16)
    taps = pltpu.VMEM((3 * chans, 9 * chans), BF16)
    dma = pltpu.SemaphoreType.DMA
    decoded = pl.pallas_call(
        functools.partial(kernel, (times, tiles, rows, chans, width)),
        out_shape=jax.ShapeDtypeStruct((frames, 3, rows, width), F32),
        in_specs=[anywhere] * 7,
        out_specs=vmem,
        scratch_shapes=[
            pltpu.VMEM(features.shape, BF16),
            pltpu.VMEM((1, chans), F32),
            pltpu.VMEM((1, chans), F32),
            pltpu.VMEM((1, chans), F32),
            pltpu.VMEM(conv_head.shape, BF16),
            raw,
            raw,
            taps,
            taps,
            pltpu.VMEM((144, 2 * chans), F32),
            ext,
            ext,
            pltpu.VMEM((2, rows + 2, 8, width), F32),
            pltpu.VMEM((rows, 8, width), F32),
            pltpu.VMEM((4, 8, width), F32),
            dma((7,)),
            dma((8,)),
            dma((8,)),
            dma((8,)),
            dma((8,)),
            dma((5,)),
            dma((5,)),
        ],
        compiler_params=pltpu.CompilerParams(
            collective_id=0, has_side_effects=True, vmem_limit_bytes=56524800
        ),
        cost_estimate=pl.CostEstimate(flops=1_100_000_000, bytes_accessed=1_300_000, transcendentals=400_000),
        name="decode",
    )(
        features,
        gain_one.reshape(1, chans),
        gain_two.reshape(1, chans),
        gain_head.reshape(1, chans),
        conv_one.reshape(9, 3 * chans, chans),
        conv_two.reshape(9, 3 * chans, chans),
        conv_head,
    )
    return jnp.transpose(decoded, (0, 2, 1, 3))


def solution(mesh):
    placed = (P("tm", "tile", None, None), P(), P(), P(), P(), P(), P())
    return jax.shard_map(
        functools.partial(local, mesh.shape["tm"], mesh.shape["tile"]),
        mesh=mesh,
        in_specs=placed,
        out_specs=P("tm", "tile", None, None),
        check_vma=False,
    )
```

time: 29.7 us -> 23.7 us (0.80)
  the two profiles are of different devices: /device:TPU:230 before, /device:TPU:238 now
where the time goes in v2:
time: 23.7 us; the launch traced here: 23.5 us
  Pallas kernels  22.2 us (94%)
  local copies, waits for them, and re-layouts  1.28 us (5%)
    pallas_call x1, Pallas kernels, local(): pl.pallas_call(functools.partial(kernel, (times, tiles, rows, chans, widt...  22.2 us
    unnamed x7, local copies, waits for them, and re-layouts  1.28 us

profile of v2, /device:TPU:238, one launch (start us, length us, event | category | flops | bytes accessed | tf_op | source)
XLA Modules:
  0.0 23.5 jit_solution(15784388220320172227)
XLA Ops:
  0.0 0.0 copy-start
  0.0 0.0 copy-start.1
  0.0 0.0 copy-start.2
  0.0 0.6 %copy-done = f32[96]{0:T(128)S(1)} copy-done((f32[96]{0:T(128)S(1)}, f32[96]{0:T(128)}, u32[]{:S(2)}) %copy-start) | copy-done | bytes 408
  0.7 0.0 copy-done.1
  0.7 0.0 copy-done.2
  0.7 22.2 %decode.1 = f32[2,3,4,128]{3,2,1,0:T(4,128)S(1)} custom-call(bf16[2,4,96,128]{3,2,1,0:T(8,128)(2,1)} %features_ref.1, f32[1,96]{1,0:T(1,128)S(1)} %bitcast.7, f32[1,96]{1,0:T(1,128)S(1)} %bitcast.8, f32[1,96]{1,0:T(1,128)S(1)} %bitcast.9, bf16[9,288,96]{2,1,0:T(8,128)(2,1)} %bitcast.10, bf16[9,288,96]{2,1,0:T(8,128)(2,1)} %bitcast.11, ...), custom_call_target="tpu_custom_call" | custom-call | flops 1100000000 | bytes 1300000 | tf_op jit(solution)/shard_map/decode/pallas_call | solution.py:341
  22.9 0.6 %copy.9 = f32[2,4,3,128]{3,1,2,0:T(4,128)} copy(f32[2,4,3,128]{3,1,2,0:T(4,128)S(1)} %bitcast.6) | data formatting | bytes 24576
Async XLA Ops:
  0.0 0.7 %copy-start = (f32[96]{0:T(128)S(1)}, f32[96]{0:T(128)}, u32[]{:S(2)}) copy-start(f32[96]{0:T(128)} %param.8) | copy-start | bytes 1156
  0.0 0.7 %copy-start.1 = (f32[96]{0:T(128)S(1)}, f32[96]{0:T(128)}, u32[]{:S(2)}) copy-start(f32[96]{0:T(128)} %param.9) | copy-start | bytes 1156
  0.0 0.7 %copy-start.2 = (f32[96]{0:T(128)S(1)}, f32[96]{0:T(128)}, u32[]{:S(2)}) copy-start(f32[96]{0:T(128)} %param.10) | copy-start | bytes 1156

commit v3 on v2

--- a/solution.py
+++ b/solution.py
@@ -113,7 +113,15 @@
     upwards = lax.rem(s, 4) < 2
     near, far = jnp.where(upwards, 1, -1), jnp.where(upwards, -1, 1)
     order = [jnp.where(upwards, rows - 1 - i, i) for i in range(rows)]
-    turns = [0, rows - 1, *range(1, rows - 1)]
+    middle = list(range(1, rows - 1))
+
+    outer = (lax.rem(s, 4) == 0) | (lax.rem(s, 4) == 3)
+    lead = jnp.where(outer & (lax.rem(t, 2) == 0), far, near)
+    lead_of_next = jnp.where(outer & (lax.rem(t, 2) == 1), far, near)
+
+    def row_from(side, i):
+        return jnp.where(side < 0, i, rows - 1 - i)
+
 
     def rows_at(at, count=1):
         return pl.ds(pl.multiple_of(at * chans, 32), count * chans)
@@ -174,15 +182,10 @@
     def await_onward(ext, sems, r):
         pl.when(older)(onward(ext, sems, r).wait_recv)
 
-    def await_row(ext, sems, i):
-        if i == 0:
-            await_onward(ext, sems, order[0])
-            await_onward(ext, sems, order[1])
-            await_edge(ext, sems, near)
-        elif i == rows - 1:
-            for r in order[2:]:
-                await_onward(ext, sems, r)
-            await_edge(ext, sems, far)
+    def await_side(ext, sems, side):
+        await_onward(ext, sems, row_from(side, 0))
+        await_onward(ext, sems, row_from(side, 1))
+        await_edge(ext, sems, side)
 
     def drain(ext, sems):
         for side in (near, far):
@@ -207,11 +210,11 @@
     pl.semaphore_wait(barrier, receivers)
     for side in (far, near):
         send_edge(ext_one, sems_one, side)
-    send_onward(ext_one, sems_one, order[0])
-    for i in range(1, rows):
-        if i < rows - 1:
-            first_act(order[i], gain_one)
-        send_onward(ext_one, sems_one, order[i])
+    for i in range(rows):
+        r = row_from(lead_of_next, i)
+        if 0 < i < rows - 1:
+            first_act(r, gain_one)
+        send_onward(ext_one, sems_one, r)
     gain_two, gain_head = spread(gain_two_ref), spread(gain_head_ref)
 
     loads[4].wait()
@@ -243,17 +246,19 @@
             for f in range(2)
         ]
 
-    for i in turns:
-        r = order[i]
-        await_row(ext_one, sems_one, i)
+    def second_act(r):
         for f, hidden in enumerate(conv_row(taps_one, ext_one, r)):
             hidden = hidden.astype(BF16).astype(F32)
             ext_two[2 + f, rows_at(r + 1)] = act(hidden, gain_two)
-        if i == 0:
-            send_edge(ext_two, sems_two, near)
-        if i == rows - 1:
-            send_edge(ext_two, sems_two, far)
-        send_onward(ext_two, sems_two, r)
+
+    for side in (lead, -lead):
+        await_side(ext_one, sems_one, side)
+        second_act(row_from(side, 0))
+        send_edge(ext_two, sems_two, side)
+        send_onward(ext_two, sems_two, row_from(side, 0))
+    for i in middle:
+        second_act(row_from(lead, i))
+        send_onward(ext_two, sems_two, row_from(lead, i))
 
     def head_edge(side, later):
         at = jnp.where(side == near, 0, rows + 1)
@@ -283,9 +288,10 @@
         for late in range(2):
             part[late, place] = shifted_sum(*[summed[late, place, c] for c in range(3)], lane)
 
-    for i in turns:
+    for i in [0, rows - 1, *middle]:
         r = order[i]
-        await_row(ext_two, sems_two, i)
+        if i in (0, rows - 1):
+            await_side(ext_two, sems_two, far if i else near)
         branch = conv_row(taps_two, ext_two, r)
         heads = []
         for f in range(2):

time: 23.7 us -> 22.6 us (0.954)
  Pallas kernels: 22.2 us -> 21.2 us
    pallas_call x1, Pallas kernels: 22.2 us -> 21.2 us  [local(): pl.pallas_call(functools.partial(kernel, (times, tiles, rows, chans, widt...]
where the time goes in v3:
time: 22.6 us; the launch traced here: 22.5 us
  Pallas kernels  21.2 us (94%)
  local copies, waits for them, and re-layouts  1.28 us (6%)
    pallas_call x1, Pallas kernels, local(): pl.pallas_call(functools.partial(kernel, (times, tiles, rows, chans, widt...  21.2 us
    unnamed x7, local copies, waits for them, and re-layouts  1.28 us

profile of v3, /device:TPU:238, one launch (start us, length us, event | category | flops | bytes accessed | tf_op | source)
XLA Modules:
  0.0 22.5 jit_solution(12964340148834139460)
XLA Ops:
  0.0 0.0 copy-start
  0.0 0.0 copy-start.1
  0.0 0.0 copy-start.2
  0.0 0.6 %copy-done = f32[96]{0:T(128)S(1)} copy-done((f32[96]{0:T(128)S(1)}, f32[96]{0:T(128)}, u32[]{:S(2)}) %copy-start) | copy-done | bytes 408
  0.7 0.0 copy-done.1
  0.7 0.0 copy-done.2
  0.7 21.2 %decode.1 = f32[2,3,4,128]{3,2,1,0:T(4,128)S(1)} custom-call(bf16[2,4,96,128]{3,2,1,0:T(8,128)(2,1)} %features_ref.1, f32[1,96]{1,0:T(1,128)S(1)} %bitcast.7, f32[1,96]{1,0:T(1,128)S(1)} %bitcast.8, f32[1,96]{1,0:T(1,128)S(1)} %bitcast.9, bf16[9,288,96]{2,1,0:T(8,128)(2,1)} %bitcast.10, bf16[9,288,96]{2,1,0:T(8,128)(2,1)} %bitcast.11, ...), custom_call_target="tpu_custom_call" | custom-call | flops 1100000000 | bytes 1300000 | tf_op jit(solution)/shard_map/decode/pallas_call | solution.py:347
  21.9 0.6 %copy.9 = f32[2,4,3,128]{3,1,2,0:T(4,128)} copy(f32[2,4,3,128]{3,1,2,0:T(4,128)S(1)} %bitcast.6) | data formatting | bytes 24576
Async XLA Ops:
  0.0 0.7 %copy-start = (f32[96]{0:T(128)S(1)}, f32[96]{0:T(128)}, u32[]{:S(2)}) copy-start(f32[96]{0:T(128)} %param.8) | copy-start | bytes 1156
  0.0 0.7 %copy-start.1 = (f32[96]{0:T(128)S(1)}, f32[96]{0:T(128)}, u32[]{:S(2)}) copy-start(f32[96]{0:T(128)} %param.9) | copy-start | bytes 1156
  0.0 0.7 %copy-start.2 = (f32[96]{0:T(128)S(1)}, f32[96]{0:T(128)}, u32[]{:S(2)}) copy-start(f32[96]{0:T(128)} %param.10) | copy-start | bytes 1156

commit v4 on v3

--- a/solution.py
+++ b/solution.py
@@ -374,18 +374,23 @@
             dma((5,)),
         ],
         compiler_params=pltpu.CompilerParams(
-            collective_id=0, has_side_effects=True, vmem_limit_bytes=56524800
+            collective_id=0, has_side_effects=True, vmem_limit_bytes=48 * 1024 * 1024
         ),
         cost_estimate=pl.CostEstimate(flops=1_100_000_000, bytes_accessed=1_300_000, transcendentals=400_000),
         name="decode",
     )(
-        features,
-        gain_one.reshape(1, chans),
-        gain_two.reshape(1, chans),
-        gain_head.reshape(1, chans),
-        conv_one.reshape(9, 3 * chans, chans),
-        conv_two.reshape(9, 3 * chans, chans),
-        conv_head,
+        *(
+            pltpu.with_memory_space_constraint(operand, pltpu.HBM)
+            for operand in (
+                features,
+                gain_one.reshape(1, chans),
+                gain_two.reshape(1, chans),
+                gain_head.reshape(1, chans),
+                conv_one.reshape(9, 3 * chans, chans),
+                conv_two.reshape(9, 3 * chans, chans),
+                conv_head,
+            )
+        )
     )
     return jnp.transpose(decoded, (0, 2, 1, 3))
 

time: 22.6 us -> 21.9 us (0.969)
  local copies, waits for them, and re-layouts: 1.28 us -> 0.6 us
    unnamed x7 -> x1, local copies, waits for them, and re-layouts: 1.28 us -> 0.6 us
where the time goes in v4:
time: 21.9 us; the launch traced here: 21.8 us
  Pallas kernels  21.2 us (97%)
  local copies, waits for them, and re-layouts  0.6 us (3%)
    pallas_call x1, Pallas kernels, local(): pl.pallas_call(functools.partial(kernel, (times, tiles, rows, chans, widt...  21.2 us
    unnamed x1, local copies, waits for them, and re-layouts  0.6 us

profile of v4, /device:TPU:238, one launch (start us, length us, event | category | flops | bytes accessed | tf_op | source)
XLA Modules:
  0.0 21.8 jit_solution(2114470073195162314)
XLA Ops:
  0.0 21.2 %decode.1 = f32[2,3,4,128]{3,2,1,0:T(4,128)S(1)} custom-call(bf16[2,4,96,128]{3,2,1,0:T(8,128)(2,1)} %features_ref.1, f32[1,96]{1,0:T(1,128)} %bitcast.9, f32[1,96]{1,0:T(1,128)} %bitcast.10, f32[1,96]{1,0:T(1,128)} %bitcast.11, bf16[9,288,96]{2,1,0:T(8,128)(2,1)} %bitcast.7, bf16[9,288,96]{2,1,0:T(8,128)(2,1)} %bitcast.8, ...), custom_call_target="tpu_custom_call" | custom-call | flops 1100000000 | bytes 1300000 | tf_op jit(solution)/shard_map/decode/pallas_call | solution.py:347
  21.2 0.6 %copy.9 = f32[2,4,3,128]{3,1,2,0:T(4,128)} copy(f32[2,4,3,128]{3,1,2,0:T(4,128)S(1)} %bitcast.6) | data formatting | bytes 24576

commit v5 on v4

--- a/solution.py
+++ b/solution.py
@@ -57,21 +57,31 @@
     recv_two,
     send_head,
     recv_head,
+    ready,
 ):
     times, tiles, rows, chans, width = sizes
     t, s = lax.axis_index("tm"), lax.axis_index("tile")
     older, newer = t > 0, t < times - 1
     above, below = s > 0, s < tiles - 1
 
+    odd = lax.rem(t, 2) == 1
+    even = jnp.logical_not(odd)
+    lent = odd & newer & (t == times // 2 - 1)
+    lent_to = even & older & (t == times // 2)
+
     senders = [
-        (older & above, (-1, -1)),
+        (older & above & jnp.logical_not(lent_to), (-1, -1)),
+        (lent & below, (1, 1)),
         (older & below, (-1, 1)),
         (above, (0, -1)),
         (below, (0, 1)),
         (older, (-1, 0)),
     ]
-    above_one, below_one, newer_one = (flag.astype(jnp.int32) for flag in (above, below, newer))
+    above_one, below_one, newer_one, lent_one, lent_to_one = (
+        flag.astype(jnp.int32) for flag in (above, below, newer, lent, lent_to)
+    )
     receivers = above_one + below_one + newer_one * (1 + above_one + below_one)
+    receivers = receivers - lent_one * below_one + lent_to_one * above_one
     barrier = pltpu.get_barrier_semaphore()
     for there, (dt, ds) in senders:
 
@@ -162,21 +172,37 @@
             (t + 1, s),
         )
 
-    odd = lax.rem(t, 2) == 1
-
-    def send_both(copy, side):
-        pl.when(newer & exists(side) & odd)(copy(side, 1).start)
+    def handed_on():
+        here = pl.ds(0, chans)
+        return remote(
+            ext_one.at[pl.ds(2, 2), here], ext_one.at[pl.ds(0, 2), here], send_one.at[3], recv_one.at[3], (t + 1, s)
+        )
+
+    def straight(ext, side):
+        there = newer & exists(side)
+        return there & jnp.logical_not(lent & (side > 0)) if ext is ext_one else there
+
+    def send_both(copy, side, there):
+        ahead = odd
+        pl.when(there & ahead)(copy(side, 1).start)
         pl.when(exists(side))(copy(side, 0).start)
-        pl.when(newer & exists(side) & jnp.logical_not(odd))(copy(side, 1).start)
+        pl.when(there & jnp.logical_not(ahead))(copy(side, 1).start)
 
     def send_edge(ext, sems, side):
-        send_both(functools.partial(edge, ext, sems), side)
+        if ext is ext_two:
+
+            @pl.when(lent & below & (side > 0))
+            def _():
+                pl.semaphore_wait(ready, 1)
+
+        send_both(functools.partial(edge, ext, sems), side, straight(ext, side))
 
     def send_onward(ext, sems, r):
         pl.when(newer)(onward(ext, sems, r).start)
 
     def await_edge(ext, sems, side):
-        pl.when(exists(side))(edge(ext, sems, -side, 0).wait_recv)
+        early = lent & (side < 0) if ext is ext_one else t < 0
+        pl.when(exists(side) & jnp.logical_not(early))(edge(ext, sems, -side, 0).wait_recv)
         pl.when(older & exists(side))(edge(ext, sems, -side, 1).wait_recv)
 
     def await_onward(ext, sems, r):
@@ -190,7 +216,7 @@
     def drain(ext, sems):
         for side in (near, far):
             pl.when(exists(side))(edge(ext, sems, side, 0).wait_send)
-            pl.when(newer & exists(side))(edge(ext, sems, side, 1).wait_send)
+            pl.when(straight(ext, side))(edge(ext, sems, side, 1).wait_send)
         for r in order:
             pl.when(newer)(onward(ext, sems, r).wait_send)
 
@@ -208,6 +234,11 @@
     first_act(order[-1], gain_one)
     first_act(order[0], gain_one)
     pl.semaphore_wait(barrier, receivers)
+
+    @pl.when(lent_to & above)
+    def _():
+        pl.semaphore_signal(ready, inc=1, device_id=(t - 1, s - 1), device_id_type=MESH)
+
     for side in (far, near):
         send_edge(ext_one, sems_one, side)
     for i in range(rows):
@@ -235,6 +266,11 @@
                     at = ((c * 3 + b) * 2 + target // 2) * 8 + (target % 2) * 4
                     taps_head[at : at + 3, f * chans : (f + 1) * chans] = piece
     head_weights = taps_head[...].astype(BF16)
+
+    @pl.when(lent & above)
+    def _():
+        edge(ext_one, sems_one, 1, 0).wait_recv()
+        handed_on().start()
 
     def conv_row(taps, ext, r):
         stacks = [jnp.concatenate([ext[f + a, rows_at(r, 3)] for a in range(3)], axis=0) for f in range(2)]
@@ -307,15 +343,16 @@
                     summed[key] = summed[key] + piece if key in summed else piece
         if i == 0:
             settle(0)
-            send_both(head_edge, near)
+            send_both(head_edge, near, newer & exists(near))
         if i == rows - 1:
             settle(rows + 1)
-            send_both(head_edge, far)
+            send_both(head_edge, far, newer & exists(far))
     for place in range(1, rows + 1):
         settle(place)
     pl.when(newer)(head_onward.start)
 
     drain(ext_one, sems_one)
+    pl.when(lent & above)(handed_on().wait_send)
     drain(ext_two, sems_two)
     pl.when(older)(head_onward.wait_recv)
     for i, r in enumerate(order):
@@ -372,6 +409,7 @@
             dma((8,)),
             dma((5,)),
             dma((5,)),
+            pltpu.SemaphoreType.REGULAR,
         ],
         compiler_params=pltpu.CompilerParams(
             collective_id=0, has_side_effects=True, vmem_limit_bytes=48 * 1024 * 1024

time: 21.9 us -> 21.7 us (level)
  Pallas kernels: 21.2 us -> 20.9 us
    pallas_call x1, Pallas kernels: 21.2 us -> 20.9 us  [local(): pl.pallas_call(functools.partial(kernel, (times, tiles, rows, chans, widt...]
where the time goes in v5:
time: 21.7 us; the launch traced here: 21.6 us
  Pallas kernels  20.9 us (96%)
  local copies, waits for them, and re-layouts  0.6 us (3%)
    pallas_call x1, Pallas kernels, local(): pl.pallas_call(functools.partial(kernel, (times, tiles, rows, chans, widt...  20.9 us
    unnamed x1, local copies, waits for them, and re-layouts  0.6 us

profile of v5, /device:TPU:238, one launch (start us, length us, event | category | flops | bytes accessed | tf_op | source)
XLA Modules:
  0.0 21.6 jit_solution(9448988543759057578)
XLA Ops:
  0.0 20.9 %decode.1 = f32[2,3,4,128]{3,2,1,0:T(4,128)S(1)} custom-call(bf16[2,4,96,128]{3,2,1,0:T(8,128)(2,1)} %features_ref.1, f32[1,96]{1,0:T(1,128)} %bitcast.9, f32[1,96]{1,0:T(1,128)} %bitcast.10, f32[1,96]{1,0:T(1,128)} %bitcast.11, bf16[9,288,96]{2,1,0:T(8,128)(2,1)} %bitcast.7, bf16[9,288,96]{2,1,0:T(8,128)(2,1)} %bitcast.8, ...), custom_call_target="tpu_custom_call" | custom-call | flops 1100000000 | bytes 1300000 | tf_op jit(solution)/shard_map/decode/pallas_call | solution.py:384
  20.9 0.6 %copy.9 = f32[2,4,3,128]{3,1,2,0:T(4,128)} copy(f32[2,4,3,128]{3,1,2,0:T(4,128)S(1)} %bitcast.6) | data formatting | bytes 24576

commit v6 on v5

--- a/solution.py
+++ b/solution.py
@@ -66,8 +66,8 @@
 
     odd = lax.rem(t, 2) == 1
     even = jnp.logical_not(odd)
-    lent = odd & newer & (t == times // 2 - 1)
-    lent_to = even & older & (t == times // 2)
+    lent = odd & newer & (t < times // 2)
+    lent_to = even & older & (t <= times // 2)
 
     senders = [
         (older & above & jnp.logical_not(lent_to), (-1, -1)),
@@ -182,8 +182,7 @@
         there = newer & exists(side)
         return there & jnp.logical_not(lent & (side > 0)) if ext is ext_one else there
 
-    def send_both(copy, side, there):
-        ahead = odd
+    def send_both(copy, side, there, ahead=odd):
         pl.when(there & ahead)(copy(side, 1).start)
         pl.when(exists(side))(copy(side, 0).start)
         pl.when(there & jnp.logical_not(ahead))(copy(side, 1).start)
@@ -195,7 +194,8 @@
             def _():
                 pl.semaphore_wait(ready, 1)
 
-        send_both(functools.partial(edge, ext, sems), side, straight(ext, side))
+        ahead = odd | (t >= times // 2) if ext is ext_one else odd
+        send_both(functools.partial(edge, ext, sems), side, straight(ext, side), ahead)
 
     def send_onward(ext, sems, r):
         pl.when(newer)(onward(ext, sems, r).start)
@@ -324,6 +324,16 @@
         for late in range(2):
             part[late, place] = shifted_sum(*[summed[late, place, c] for c in range(3)], lane)
 
+    def collect(i, product):
+        for c in range(3):
+            for b in range(3):
+                for late in range(2):
+                    at = ((c * 3 + b) * 2 + late) * 8
+                    piece = product[at : at + 8]
+                    key = (late, i + 2 - b, c)
+                    summed[key] = summed[key] + piece if key in summed else piece
+
+    waiting = []
     for i in [0, rows - 1, *middle]:
         r = order[i]
         if i in (0, rows - 1):
@@ -333,14 +343,17 @@
         for f in range(2):
             total = (own[f, r].astype(F32) + branch[f]).astype(BF16).astype(F32)
             heads.append(act(total, gain_head))
-        product = jnp.dot(head_weights, jnp.concatenate(heads, axis=0), preferred_element_type=F32)
-        for c in range(3):
-            for b in range(3):
-                for late in range(2):
-                    at = ((c * 3 + b) * 2 + late) * 8
-                    piece = product[at : at + 8]
-                    key = (late, i + 2 - b, c)
-                    summed[key] = summed[key] + piece if key in summed else piece
+        heads = jnp.concatenate(heads, axis=0)
+        if i in middle:
+            waiting.append(heads)
+            if i != middle[-1]:
+                continue
+            product = jnp.dot(head_weights, jnp.concatenate(waiting, axis=1), preferred_element_type=F32)
+            for n, at in enumerate(middle):
+                collect(at, product[:, n * width : (n + 1) * width])
+            continue
+        product = jnp.dot(head_weights, heads, preferred_element_type=F32)
+        collect(i, product)
         if i == 0:
             settle(0)
             send_both(head_edge, near, newer & exists(near))

time: 21.7 us -> 21.6 us (level)
  no operation moved by 1% of the time
where the time goes in v6:
time: 21.6 us; the launch traced here: 21.5 us
  Pallas kernels  20.9 us (97%)
  local copies, waits for them, and re-layouts  0.6 us (3%)
    pallas_call x1, Pallas kernels, local(): pl.pallas_call(functools.partial(kernel, (times, tiles, rows, chans, widt...  20.9 us
    unnamed x1, local copies, waits for them, and re-layouts  0.6 us

profile of v6, /device:TPU:238, one launch (start us, length us, event | category | flops | bytes accessed | tf_op | source)
XLA Modules:
  0.0 21.5 jit_solution(1562754393817672919)
XLA Ops:
  0.0 20.9 %decode.1 = f32[2,3,4,128]{3,2,1,0:T(4,128)S(1)} custom-call(bf16[2,4,96,128]{3,2,1,0:T(8,128)(2,1)} %features_ref.1, f32[1,96]{1,0:T(1,128)} %bitcast.9, f32[1,96]{1,0:T(1,128)} %bitcast.10, f32[1,96]{1,0:T(1,128)} %bitcast.11, bf16[9,288,96]{2,1,0:T(8,128)(2,1)} %bitcast.7, bf16[9,288,96]{2,1,0:T(8,128)(2,1)} %bitcast.8, ...), custom_call_target="tpu_custom_call" | custom-call | flops 1100000000 | bytes 1300000 | tf_op jit(solution)/shard_map/decode/pallas_call | solution.py:397
  20.9 0.6 %copy.9 = f32[2,4,3,128]{3,1,2,0:T(4,128)} copy(f32[2,4,3,128]{3,1,2,0:T(4,128)S(1)} %bitcast.6) | data formatting | bytes 24576

commit v7 on v5

--- a/solution.py
+++ b/solution.py
@@ -324,16 +324,7 @@
         for late in range(2):
             part[late, place] = shifted_sum(*[summed[late, place, c] for c in range(3)], lane)
 
-    for i in [0, rows - 1, *middle]:
-        r = order[i]
-        if i in (0, rows - 1):
-            await_side(ext_two, sems_two, far if i else near)
-        branch = conv_row(taps_two, ext_two, r)
-        heads = []
-        for f in range(2):
-            total = (own[f, r].astype(F32) + branch[f]).astype(BF16).astype(F32)
-            heads.append(act(total, gain_head))
-        product = jnp.dot(head_weights, jnp.concatenate(heads, axis=0), preferred_element_type=F32)
+    def collect(i, product):
         for c in range(3):
             for b in range(3):
                 for late in range(2):
@@ -341,12 +332,32 @@
                     piece = product[at : at + 8]
                     key = (late, i + 2 - b, c)
                     summed[key] = summed[key] + piece if key in summed else piece
-        if i == 0:
-            settle(0)
-            send_both(head_edge, near, newer & exists(near))
-        if i == rows - 1:
-            settle(rows + 1)
-            send_both(head_edge, far, newer & exists(far))
+
+    def heads_of(i):
+        r = order[i]
+        branch = conv_row(taps_two, ext_two, r)
+        heads = []
+        for f in range(2):
+            total = (own[f, r].astype(F32) + branch[f]).astype(BF16).astype(F32)
+            heads.append(act(total, gain_head))
+        return jnp.concatenate(heads, axis=0)
+
+    def add_heads(pair, heads):
+        product = jnp.dot(head_weights, jnp.concatenate(heads, axis=1), preferred_element_type=F32)
+        for n, i in enumerate(pair):
+            collect(i, product[:, n * width : (n + 1) * width])
+
+    edges = [0, rows - 1]
+    heads = []
+    for i in edges:
+        await_side(ext_two, sems_two, far if i else near)
+        heads.append(heads_of(i))
+    add_heads(edges, heads)
+    settle(rows + 1)
+    send_both(head_edge, far, newer & exists(far))
+    settle(0)
+    send_both(head_edge, near, newer & exists(near))
+    add_heads(middle, [heads_of(i) for i in middle])
     for place in range(1, rows + 1):
         settle(place)
     pl.when(newer)(head_onward.start)

time: 21.7 us -> 21.7 us (level)
  no operation moved by 1% of the time
where the time goes in v7:
time: 21.7 us; the launch traced here: 21.6 us
  Pallas kernels  20.9 us (96%)
  local copies, waits for them, and re-layouts  0.6 us (3%)
    pallas_call x1, Pallas kernels, local(): pl.pallas_call(functools.partial(kernel, (times, tiles, rows, chans, widt...  20.9 us
    unnamed x1, local copies, waits for them, and re-layouts  0.6 us

profile of v7, /device:TPU:238, one launch (start us, length us, event | category | flops | bytes accessed | tf_op | source)
XLA Modules:
  0.0 21.6 jit_solution(10681884815817401055)
XLA Ops:
  0.0 20.9 %decode.1 = f32[2,3,4,128]{3,2,1,0:T(4,128)S(1)} custom-call(bf16[2,4,96,128]{3,2,1,0:T(8,128)(2,1)} %features_ref.1, f32[1,96]{1,0:T(1,128)} %bitcast.9, f32[1,96]{1,0:T(1,128)} %bitcast.10, f32[1,96]{1,0:T(1,128)} %bitcast.11, bf16[9,288,96]{2,1,0:T(8,128)(2,1)} %bitcast.7, bf16[9,288,96]{2,1,0:T(8,128)(2,1)} %bitcast.8, ...), custom_call_target="tpu_custom_call" | custom-call | flops 1100000000 | bytes 1300000 | tf_op jit(solution)/shard_map/decode/pallas_call | solution.py:395
  20.9 0.6 %copy.9 = f32[2,4,3,128]{3,1,2,0:T(4,128)} copy(f32[2,4,3,128]{3,1,2,0:T(4,128)S(1)} %bitcast.6) | data formatting | bytes 24576

commit v8 on v7

--- a/solution.py
+++ b/solution.py
@@ -182,8 +182,7 @@
         there = newer & exists(side)
         return there & jnp.logical_not(lent & (side > 0)) if ext is ext_one else there
 
-    def send_both(copy, side, there):
-        ahead = odd
+    def send_both(copy, side, there, ahead=odd):
         pl.when(there & ahead)(copy(side, 1).start)
         pl.when(exists(side))(copy(side, 0).start)
         pl.when(there & jnp.logical_not(ahead))(copy(side, 1).start)
@@ -195,7 +194,8 @@
             def _():
                 pl.semaphore_wait(ready, 1)
 
-        send_both(functools.partial(edge, ext, sems), side, straight(ext, side))
+        ahead = odd | (t >= times // 2) if ext is ext_one else odd
+        send_both(functools.partial(edge, ext, sems), side, straight(ext, side), ahead)
 
     def send_onward(ext, sems, r):
         pl.when(newer)(onward(ext, sems, r).start)

time: 21.7 us -> 21.7 us (level)
  no operation moved by 1% of the time
where the time goes in v8:
time: 21.7 us; the launch traced here: 21.6 us
  Pallas kernels  20.9 us (96%)
  local copies, waits for them, and re-layouts  0.6 us (3%)
    pallas_call x1, Pallas kernels, local(): pl.pallas_call(functools.partial(kernel, (times, tiles, rows, chans, widt...  20.9 us
    unnamed x1, local copies, waits for them, and re-layouts  0.6 us

profile of v8, /device:TPU:238, one launch (start us, length us, event | category | flops | bytes accessed | tf_op | source)
XLA Modules:
  0.0 21.6 jit_solution(11831854785304709527)
XLA Ops:
  0.0 20.9 %decode.1 = f32[2,3,4,128]{3,2,1,0:T(4,128)S(1)} custom-call(bf16[2,4,96,128]{3,2,1,0:T(8,128)(2,1)} %features_ref.1, f32[1,96]{1,0:T(1,128)} %bitcast.9, f32[1,96]{1,0:T(1,128)} %bitcast.10, f32[1,96]{1,0:T(1,128)} %bitcast.11, bf16[9,288,96]{2,1,0:T(8,128)(2,1)} %bitcast.7, bf16[9,288,96]{2,1,0:T(8,128)(2,1)} %bitcast.8, ...), custom_call_target="tpu_custom_call" | custom-call | flops 1100000000 | bytes 1300000 | tf_op jit(solution)/shard_map/decode/pallas_call | solution.py:395
  20.9 0.6 %copy.9 = f32[2,4,3,128]{3,1,2,0:T(4,128)} copy(f32[2,4,3,128]{3,1,2,0:T(4,128)S(1)} %bitcast.6) | data formatting | bytes 24576
